TPU v7x, 32 devices: a whole 2x2x4 slice. The times are simulated.
32 devices in a mesh: dp: 4 (over y, core), tile: 8 (over z, x).
Axes of the slice: x: 2, y: 2, z: 4, core: 2. Of those that a mesh axis runs over, the one named last changes fastest.
Arguments:
- video_in: bfloat16 [4, 16, 32, 8, 256], P('dp', None, 'tile'), may hold values from -12 to 12
- clip_lengths: int32 [4, 6], P('dp'), may hold values from 1 to 5, 16 in all within a row
- norm_gain: float32 [256], replicated, may hold values from 0.1 to 1.9
- norm_bias: float32 [256], replicated, may hold values from -3 to 3
- spatial_weight: bfloat16 [3, 3, 256, 256], replicated, may hold values from -0.125 to 0.125
- temporal_weight: bfloat16 [3, 256, 256], replicated, may hold values from -0.21875 to 0.21875
- cotangent: bfloat16 [4, 16, 32, 8, 256], P('dp', 'tile'), may hold values from -6 to 6
Outputs:
- encoded: bfloat16 [4, 16, 32, 8, 256], P('dp', 'tile')
- spatial_grad: float32 [3, 3, 256, 256], replicated
- temporal_grad: float32 [3, 256, 256], replicated
Inputs may be any that keep to these rules, and one draw needn't show every extreme that they name: `clip_lengths`: the lengths of each batch sum to 16.
All inputs are finite; a program needn't handle non-finite values.
Results may differ from a plain program's by a relative error of at most 0.005.
Values may be sent and summed in bfloat16 or wider, within the bound.
A program may use at most 64 MiB of HBM per device.

v0:
```python
import math

import jax
import jax.numpy as jnp
from jax import lax
from jax.sharding import PartitionSpec as P

GROUPS = 32


norm_eps = 1e-05


def extended(cells, sides, width):
    for axis, dim in sides:
        count = lax.axis_size(axis)
        ends = count - 1
        head = lax.slice_in_dim(cells, 0, width, axis=dim)
        tail = lax.slice_in_dim(cells, cells.shape[dim] - width, cells.shape[dim], axis=dim)
        cells = jnp.concatenate(
            [
                lax.ppermute(tail, axis, [(i, (i + 1) % count) for i in range(ends)]),
                cells,
                lax.ppermute(head, axis, [((i + 1) % count, i) for i in range(ends)]),
            ],
            axis=dim,
        )
    return cells


def from_behind(shard, axis, by):
    peers = lax.axis_size(axis)
    pairs = [(i, i + by) for i in range(peers) if 0 <= i + by < peers]
    return lax.ppermute(shard, axis, pairs)


def clip_tables(lengths, frame_total):
    clip_ends = jnp.cumsum(lengths)
    clip_starts = clip_ends - lengths
    frame_ids = jnp.arange(frame_total, dtype=jnp.int32)
    membership = (frame_ids[:, None] >= clip_starts[None, :]) & (
        frame_ids[:, None] < clip_ends[None, :]
    )
    clip_first = jnp.sum(jnp.where(membership, clip_starts[None, :], 0), axis=1)
    return (membership.astype(jnp.float32), frame_ids - clip_first)


def group_total(onehot, frame_term, group_count):
    clip_term = jnp.dot(onehot.T, frame_term, precision=lax.Precision.HIGHEST)
    return clip_term.reshape(clip_term.shape[0], group_count, -1).sum(axis=2)


def spread_back(onehot, clip_group, channels):
    per_channel = jnp.repeat(clip_group, channels // clip_group.shape[1], axis=1)
    return jnp.dot(onehot, per_channel, precision=lax.Precision.HIGHEST)


def patch_columns(padded, strip_rows, frame_width):
    pieces = [
        padded[:, row_step : row_step + strip_rows, col_step : col_step + frame_width, :]
        for row_step in range(3)
        for col_step in range(3)
    ]
    return jnp.concatenate(pieces, axis=-1).reshape(-1, 9 * padded.shape[-1])


def earlier_stack(block_ext, pos_here):
    frame_count = pos_here.shape[0]
    stacked = []
    for offset in range(3):
        keep = (pos_here >= offset)[:, None, None, None]
        window = block_ext[2 - offset : 2 - offset + frame_count]
        stacked.append(jnp.where(keep, window, jnp.zeros_like(window)))
    return jnp.concatenate(stacked, axis=-1)


def later_stack(cot_ext, pos_ahead):
    frame_count = pos_ahead.shape[0] - 2
    stacked = []
    for offset in range(3):
        keep = (pos_ahead[offset : offset + frame_count] >= offset)[:, None, None, None]
        window = cot_ext[offset : offset + frame_count]
        stacked.append(jnp.where(keep, window, jnp.zeros_like(window)))
    return jnp.concatenate(stacked, axis=-1)


def contract_rows(left, right):
    return lax.dot_general(
        left, right, (((0,), (0,)), ((), ())), preferred_element_type=jnp.float32
    )


def temporal_pass(block_ext, cot_ext, pos_here, pos_ahead, temporal_weight):
    channels = temporal_weight.shape[1]
    frame_count = pos_here.shape[0]
    earlier = earlier_stack(block_ext, pos_here).reshape(-1, 3 * channels)
    block_now = block_ext[2:]
    lifted = jnp.dot(
        earlier, temporal_weight.reshape(3 * channels, channels), preferred_element_type=jnp.float32
    )
    encoded = (block_now.astype(jnp.float32) + lifted.reshape(block_now.shape)).astype(jnp.bfloat16)
    cot_now = cot_ext[:frame_count]
    later_cot = later_stack(cot_ext, pos_ahead).reshape(-1, 3 * channels)
    back_weight = jnp.transpose(temporal_weight, (0, 2, 1)).reshape(3 * channels, channels)
    pulled = jnp.dot(later_cot, back_weight, preferred_element_type=jnp.float32)
    grad_block = (cot_now.astype(jnp.float32) + pulled.reshape(cot_now.shape)).astype(jnp.bfloat16)
    temporal_term = contract_rows(earlier, cot_now.reshape(-1, channels))
    return (encoded, grad_block, temporal_term)


def on_device(
    video_in, clip_lengths, norm_gain, norm_bias, spatial_weight, temporal_weight, cotangent
):
    tile_count = lax.axis_size("tile")
    frames = video_in.shape[1]
    strip_rows = video_in.shape[2]
    frame_width = video_in.shape[3]
    channels = video_in.shape[4]
    height = strip_rows * tile_count
    frame_dev = frames // tile_count
    lengths = clip_lengths[0]
    onehot, position = clip_tables(lengths, frames)
    local_vals = video_in[0].astype(jnp.float32)
    per_group = channels // GROUPS
    counts = lengths.astype(jnp.float32) * (height * frame_width * per_group)
    frame_sum = jnp.sum(local_vals, axis=(1, 2))
    totals, squares = lax.psum(
        (
            group_total(onehot, frame_sum, GROUPS),
            group_total(onehot, jnp.sum(local_vals * local_vals, axis=(1, 2)), GROUPS),
        ),
        "tile",
    )
    clip_mean = totals / counts[:, None]
    clip_var = squares / counts[:, None] - clip_mean * clip_mean
    centered = local_vals - spread_back(onehot, clip_mean, channels)[:, None, None, :]
    rstd_frame = spread_back(onehot, lax.rsqrt(clip_var + norm_eps), channels)
    normed = centered * rstd_frame[:, None, None, :] * norm_gain + norm_bias
    active = jax.nn.silu(normed).astype(jnp.bfloat16)
    padded = extended(active, (("tile", 1),), 1)
    padded = jnp.pad(padded, ((0, 0), (0, 0), (1, 1), (0, 0)))
    columns = patch_columns(padded, strip_rows, frame_width)
    conv_out = jnp.dot(
        columns, spatial_weight.reshape(9 * channels, channels), preferred_element_type=jnp.float32
    )
    block_out = (local_vals + conv_out.reshape(local_vals.shape)).astype(jnp.bfloat16)
    block_time = lax.all_to_all(block_out[None], "tile", split_axis=1, concat_axis=2, tiled=True)[0]
    before_frames = from_behind(block_time, "tile", 1)
    block_ext = jnp.concatenate([before_frames, block_time], axis=0)
    after_frames = from_behind(cotangent[0, :2], "tile", -1)
    cot_ext = jnp.concatenate([cotangent[0], after_frames], axis=0)
    first_frame = lax.axis_index("tile") * frame_dev
    pos_padded = jnp.concatenate([position, jnp.zeros((2,), jnp.int32)], axis=0)
    pos_here = lax.dynamic_slice_in_dim(position, first_frame, frame_dev)
    pos_ahead = lax.dynamic_slice_in_dim(pos_padded, first_frame, frame_dev + 2)
    encoded_time, grad_time, temporal_term = temporal_pass(
        block_ext, cot_ext, pos_here, pos_ahead, temporal_weight
    )
    encoded = encoded_time[None]
    grad_block = lax.all_to_all(grad_time[None], "tile", split_axis=2, concat_axis=1, tiled=True)[0]
    spatial_term = contract_rows(columns, grad_block.reshape(-1, channels))
    pixel_total = lax.axis_size("dp") * frames * height * frame_width
    grad_scale = 1.0 / math.sqrt(pixel_total)
    spatial_grad, temporal_grad = lax.psum(
        (spatial_term * grad_scale, temporal_term * grad_scale), ("dp", "tile")
    )
    return (
        encoded,
        spatial_grad.reshape(3, 3, channels, channels),
        temporal_grad.reshape(3, channels, channels),
    )


def solution(mesh):
    return jax.shard_map(
        on_device,
        mesh=mesh,
        in_specs=(
            P("dp", None, "tile", None, None),
            P("dp", None),
            P(),
            P(),
            P(),
            P(),
            P("dp", "tile", None, None, None),
        ),
        out_specs=(P("dp", "tile", None, None, None), P(), P()),
        check_vma=False,
    )
```

profile of v0, /device:TPU:1, one launch (start us, length us, event | category | flops | bytes accessed | tf_op | source)
XLA Modules:
  0.0 223.8 jit_solution(18196637187773866742)
XLA Ops:
  7.2 1.1 fusion.28
  8.3 1.0 convert_reduce_fusion
  9.3 0.7 multiply_bitcast_fusion
  10.0 0.8 reduce-window.4
  10.8 0.7 fusion.38
  11.7 0.4 convolution_reduce_fusion.1
  12.1 0.4 convolution_reduce_fusion
  12.5 19.0 %all-reduce.3 = (f32[6,32]{1,0:T(8,128)S(1)}, f32[6,32]{1,0:T(8,128)S(1)}) all-reduce(f32[6,32]{1,0:T(8,128)S(1)} %convolution_reduce_fusion, f32[6,32]{1,0:T(8,128)S(1)} %convolution_reduce_fusion.1), channel_id=1, replica_groups=mesh['dp'=4,'tile'=8] {'tile'}, use_global_device_ids=true, to_apply=%region_6.7 | all-reduce | flops 384 | bytes 3072 | tf_op jit(solution)/shard_map/psum | solution.py:127
  31.8 0.3 fusion.43
  32.3 0.3 fusion.41
  32.5 1.2 fusion.27
  33.7 1.3 collective-permute-start
  35.0 1.3 collective-permute-start.1
  36.3 1.3 collective-permute-start.3
  37.9 2.1 collective-permute-done.1
  40.0 0.4 fusion.11
  40.6 0.2 constant_dynamic-update-slice_fusion
  41.1 1.4 copy-done.5
  42.5 1.5 fusion.6
  44.0 3.4 %all-to-all-start = ((bf16[1,16,4,8,256]{4,3,2,0,1:T(8,128)(2,1)}), bf16[1,16,4,8,256]{4,3,2,0,1:T(8,128)(2,1)S(1)}, u32[]{:S(2)}, u32[]{:S(2)}) async-start(bf16[1,16,4,8,256]{4,3,2,0,1:T(8,128)(2,1)} %fusion.6), calls=%async_computation | async-start | bytes 524288 | tf_op jit(solution)/shard_map/all_to_all | solution.py:147
  47.8 0.4 fusion.4
  48.2 0.7 copy.31
  48.9 5.5 %all-to-all-done = bf16[1,16,4,8,256]{4,3,2,0,1:T(8,128)(2,1)S(1)} async-done(((bf16[1,16,4,8,256]{4,3,2,0,1:T(8,128)(2,1)}), bf16[1,16,4,8,256]{4,3,2,0,1:T(8,128)(2,1)S(1)}, u32[]{:S(2)}, u32[]{:S(2)}) %all-to-all-start) | async-done | bytes 262176 | tf_op jit(solution)/shard_map/all_to_all | solution.py:147
  54.4 3.4 %all-to-all-start.1 = ((bf16[1,2,32,8,256]{4,3,1,0,2:T(8,128)(2,1)}), bf16[1,2,32,8,256]{4,3,1,0,2:T(8,128)(2,1)S(1)}, u32[]{:S(2)}, u32[]{:S(2)}) async-start(bf16[1,2,32,8,256]{4,3,1,0,2:T(8,128)(2,1)} %copy.31), calls=%async_computation.1 | async-start | bytes 524288 | tf_op jit(solution)/shard_map/all_to_all | solution.py:160
  58.0 3.2 %collective-permute-start.2 = (bf16[2,32,8,256]{3,2,1,0:T(8,128)(2,1)S(1)}, bf16[2,32,8,256]{3,2,1,0:T(8,128)(2,1)S(1)}, u32[]{:S(2)}, u32[]{:S(2)}) collective-permute-start(bf16[2,32,8,256]{3,2,1,0:T(8,128)(2,1)S(1)} %bitcast.111), channel_id=1, source_target_pairs={{0,1},{1,2},{2,3},{3,4},{4,5},{5,6},{6,7},{8,9},{9,10},{10,11},{11... | collective-permute-start | bytes 786440 | tf_op jit(solution)/shard_map/ppermute | solution.py:34
  61.2 3.6 %all-to-all-done.1 = bf16[1,2,32,8,256]{4,3,1,0,2:T(8,128)(2,1)S(1)} async-done(((bf16[1,2,32,8,256]{4,3,1,0,2:T(8,128)(2,1)}), bf16[1,2,32,8,256]{4,3,1,0,2:T(8,128)(2,1)S(1)}, u32[]{:S(2)}, u32[]{:S(2)}) %all-to-all-start.1) | async-done | bytes 262176 | tf_op jit(solution)/shard_map/all_to_all | solution.py:160
  64.9 3.9 %convolution_multiply_fusion = f32[2304,256]{1,0:T(8,128)} fusion(bf16[512,2304]{1,0:T(8,128)(2,1)} %bitcast.121, bf16[512,256]{1,0:T(8,128)(2,1)S(1)} %bitcast.118), kind=kOutput, calls=%fused_computation | convolution fusion | flops 604569600 | bytes 4980736 | tf_op jit(solution)/shard_map/dot_general | solution.py:88
  68.9 1.3 convolution_multiply_fusion.1
  70.3 1.1 fusion.5
  71.3 141.5 %all-reduce.6.cloned.1.call-done = (f32[3,3,256,256]{3,2,1,0:T(8,128)}, f32[3,256,256]{2,1,0:T(8,128)}) async-done(((f32[3,3,256,256]{3,2,1,0:T(8,128)}, f32[3,256,256]{2,1,0:T(8,128)}), (f32[3,3,256,256]{3,2,1,0:T(8,128)}, f32[3,256,256]{2,1,0:T(8,128)})) %all-reduce.6.cloned.1.call-update) | async-done | bytes 3145744 | tf_op jit(solution)/shard_map/psum | solution.py:164
  212.8 3.3 %copy.51 = f32[3,3,256,256]{3,2,1,0:T(8,128)} copy(f32[3,3,256,256]{3,2,1,0:T(8,128)} %get-tuple-element.23) | data formatting | bytes 4718592
  216.1 0.9 copy.52
  (49 shorter events, 2.1 us)
Async XLA Ops:
  7.2 33.9 %copy-start = (bf16[3,3,256,256]{3,2,1,0:T(8,128)(2,1)S(1)}, bf16[3,3,256,256]{3,2,1,0:T(8,128)(2,1)}, u32[]{:S(2)}) copy-start(bf16[3,3,256,256]{3,2,1,0:T(8,128)(2,1)} %param.11) | copy-start | bytes 3538948
  7.2 29.1 %copy-start.2 = (bf16[1,2,32,8,256]{4,3,2,1,0:T(8,128)(2,1)S(1)}, bf16[1,2,32,8,256]{4,3,2,1,0:T(8,128)(2,1)}, u32[]{:S(2)}) copy-start(bf16[1,2,32,8,256]{4,3,2,1,0:T(8,128)(2,1)} %param.13) | copy-start | bytes 786436
  31.6 8.9 %copy-start.1 = (bf16[1,16,4,8,256]{4,3,2,1,0:T(8,128)(2,1)S(1)}, bf16[1,16,4,8,256]{4,3,2,1,0:T(8,128)(2,1)}, u32[]{:S(2)}) copy-start(bf16[1,16,4,8,256]{4,3,2,1,0:T(8,128)(2,1)} %param.7) | copy-start | bytes 786436
  31.7 8.9 %copy-start.6 = (f32[256]{0:T(256)S(1)}, f32[256]{0:T(256)}, u32[]{:S(2)}) copy-start(f32[256]{0:T(256)} %param.10) | copy-start | bytes 3076
  31.7 8.9 %copy-start.7 = (f32[256]{0:T(256)S(1)}, f32[256]{0:T(256)}, u32[]{:S(2)}) copy-start(f32[256]{0:T(256)} %param.9) | copy-start | bytes 3076
  33.7 4.2 %collective-permute-start = (bf16[16,1,8,256]{3,2,1,0:T(8,128)(2,1)S(1)}, bf16[16,1,8,256]{3,2,1,0:T(8,128)(2,1)S(1)}, u32[]{:S(2)}, u32[]{:S(2)}) collective-permute-start(bf16[16,1,8,256]{3,2,1,0:T(8,128)(2,1)S(1)} %get-tuple-element.12), channel_id=1, source_target_pairs={{0,1},{1,2},{2,3},{3,4},{4,5},{5,6},{6,7},{8,9},{9,10},{10,11},{11... | collective-permute-start | bytes 196616 | tf_op jit(solution)/shard_map/ppermute | solution.py:22
  35.0 5.0 %collective-permute-start.1 = (bf16[16,1,8,256]{3,2,1,0:T(8,128)(2,1)S(1)}, bf16[16,1,8,256]{3,2,1,0:T(8,128)(2,1)S(1)}, u32[]{:S(2)}, u32[]{:S(2)}) collective-permute-start(bf16[16,1,8,256]{3,2,1,0:T(8,128)(2,1)S(1)} %get-tuple-element.13), channel_id=1, source_target_pairs={{1,0},{2,1},{3,2},{4,3},{5,4},{6,5},{7,6},{9,8},{10,9},{11,10},{12... | collective-permute-start | bytes 196616 | tf_op jit(solution)/shard_map/ppermute | solution.py:24
  36.3 11.3 %collective-permute-start.3 = (bf16[2,32,8,256]{3,2,1,0:T(8,128)(2,1)S(1)}, bf16[2,32,8,256]{3,2,1,0:T(8,128)(2,1)S(1)}, u32[]{:S(2)}, u32[]{:S(2)}) collective-permute-start(bf16[2,32,8,256]{3,2,1,0:T(8,128)(2,1)S(1)} %bitcast.105), channel_id=1, source_target_pairs={{1,0},{2,1},{3,2},{4,3},{5,4},{6,5},{7,6},{9,8},{10,9},{11,10},{12... | collective-permute-start | bytes 786440 | tf_op jit(solution)/shard_map/ppermute | solution.py:34
  41.0 1.4 copy-start.5
  42.5 5.0 %copy-start.4 = (bf16[3,256,256]{2,1,0:T(8,128)(2,1)S(1)}, bf16[3,256,256]{2,1,0:T(8,128)(2,1)}, u32[]{:S(2)}) copy-start(bf16[3,256,256]{2,1,0:T(8,128)(2,1)} %param.12) | copy-start | bytes 1179652
  44.0 10.4 %all-to-all-start = ((bf16[1,16,4,8,256]{4,3,2,0,1:T(8,128)(2,1)}), bf16[1,16,4,8,256]{4,3,2,0,1:T(8,128)(2,1)S(1)}, u32[]{:S(2)}, u32[]{:S(2)}) async-start(bf16[1,16,4,8,256]{4,3,2,0,1:T(8,128)(2,1)} %fusion.6), calls=%async_computation | async-start | bytes 524288 | tf_op jit(solution)/shard_map/all_to_all | solution.py:147
  54.4 10.4 %all-to-all-start.1 = ((bf16[1,2,32,8,256]{4,3,1,0,2:T(8,128)(2,1)}), bf16[1,2,32,8,256]{4,3,1,0,2:T(8,128)(2,1)S(1)}, u32[]{:S(2)}, u32[]{:S(2)}) async-start(bf16[1,2,32,8,256]{4,3,1,0,2:T(8,128)(2,1)} %copy.31), calls=%async_computation.1 | async-start | bytes 524288 | tf_op jit(solution)/shard_map/all_to_all | solution.py:160
  57.8 155.0 %all-reduce.6.cloned.1.call-start = ((), (), s32[]{:S(2)}) async-start(), calls=%async_computation.2 | async-start | bytes 6291456 | tf_op jit(solution)/shard_map/psum | solution.py:164
  58.0 10.8 %collective-permute-start.2 = (bf16[2,32,8,256]{3,2,1,0:T(8,128)(2,1)S(1)}, bf16[2,32,8,256]{3,2,1,0:T(8,128)(2,1)S(1)}, u32[]{:S(2)}, u32[]{:S(2)}) collective-permute-start(bf16[2,32,8,256]{3,2,1,0:T(8,128)(2,1)S(1)} %bitcast.111), channel_id=1, source_target_pairs={{0,1},{1,2},{2,3},{3,4},{4,5},{5,6},{6,7},{8,9},{9,10},{10,11},{11... | collective-permute-start | bytes 786440 | tf_op jit(solution)/shard_map/ppermute | solution.py:34
  212.8 3.3 %copy-start.3 = (f32[3,256,256]{2,1,0:T(8,128)S(1)}, f32[3,256,256]{2,1,0:T(8,128)}, u32[]{:S(2)}) copy-start(f32[3,256,256]{2,1,0:T(8,128)} %get-tuple-element.24) | copy-start | bytes 2359300
Sparse Core Ops, SparseCore 0:
  70.4 142.3 all-reduce.5
where the time goes:
time: 226 us; the launch traced here: 224 us
  waiting for transfers between devices  153 us (68%)
  blocking collectives  19 us (8%)
  between operations  14.4 us (6%)
  starting transfers between devices  14 us (6%)
  matrix products  9.43 us (4%)
  local copies, waits for them, and re-layouts  7.54 us (3%)
  other arithmetic  6.79 us (3%)
    psum x1, waiting for transfers between devices, on_device(): lax.psum((spatial_term * grad_scale, temporal_term * grad_scale), ('dp',...  141 us
    psum x1, blocking collectives, on_device(): lax.psum((group_total(onehot, frame_sum, GROUPS), group_total(onehot, jnp...  19 us
    unnamed x24, local copies, waits for them, and re-layouts  6 us
    all_to_all x1, waiting for transfers between devices, on_device(): lax.all_to_all(block_out[None], 'tile', split_axis=1, concat_axis=2, tile...  5.5 us
    dot_general x2, matrix products, contract_rows(): lax.dot_general(left, right, (((0,), (0,)), ((), ())), preferred_element_...  5.18 us
  transfers between devices with their start and end apart: 7, of which 4 were waited for; matrix products, arithmetic and copies ran while one was open for 4% of the time, Pallas kernels for 0%

commit v1 on v0

v1 whole, which is shorter than its diff:
```python
import functools
import math

import jax
import jax.numpy as jnp
from jax import lax
from jax.experimental import pallas as pl
from jax.experimental.pallas import tpu as pltpu
from jax.sharding import PartitionSpec as P

GROUPS = 32
MESH = pl.DeviceIdType.MESH
norm_eps = 1e-05


def remote(src, dst, send, recv, peer):
    return pltpu.make_async_remote_copy(
        src_ref=src,
        dst_ref=dst,
        send_sem=send,
        recv_sem=recv,
        device_id=peer,
        device_id_type=MESH,
    )


def exchange_kernel(
    tiles,
    video_ref,
    top_ref,
    bot_ref,
    cot_ref,
    stats_ref,
    rows_ref,
    above_ref,
    below_ref,
    mine,
    theirs,
    stat_send,
    stat_recv,
    halo_send,
    halo_recv,
    cot_send,
    cot_recv,
):
    dp, me = lax.axis_index("dp"), lax.axis_index("tile")
    frames, cells, channels = video_ref.shape
    frame_dev = cot_ref.shape[0]
    barrier = pltpu.get_barrier_semaphore()
    peers = [lax.rem(me + k, tiles) for k in range(1, tiles)]
    for peer in peers:
        pl.semaphore_signal(barrier, inc=1, device_id=(dp, peer), device_id_type=MESH)
    values = video_ref[...].astype(jnp.float32)
    sums = jnp.concatenate(
        [jnp.sum(values, axis=1), jnp.sum(values * values, axis=1)], axis=0
    )
    lanes = mine.shape[1]
    per_group = channels // GROUPS
    member = lax.broadcasted_iota(jnp.int32, (channels, lanes), 0) // per_group
    group = lax.broadcasted_iota(jnp.int32, (channels, lanes), 1)
    pick = jnp.where(member == group, 1.0, 0.0).astype(jnp.float32)
    mine[...] = jnp.dot(
        sums, pick, precision=lax.Precision.HIGHEST, preferred_element_type=jnp.float32
    )
    pl.semaphore_wait(barrier, tiles - 1)
    stats = []
    for k, peer in enumerate(peers):
        copy = remote(mine, theirs.at[k], stat_send.at[k], stat_recv.at[k], (dp, peer))
        copy.start()
        stats.append(copy)
    up = remote(top_ref, below_ref, halo_send.at[0], halo_recv.at[0], (dp, me - 1))
    down = remote(bot_ref, above_ref, halo_send.at[1], halo_recv.at[1], (dp, me + 1))

    @pl.when(me > 0)
    def _():
        up.start()

    @pl.when(me < tiles - 1)
    def _():
        down.start()

    moves = []
    for k, peer in enumerate(peers):
        copy = remote(
            cot_ref.at[:, pl.ds(peer * cells, cells)],
            rows_ref.at[pl.ds(me * frame_dev, frame_dev)],
            cot_send.at[k],
            cot_recv.at[k],
            (dp, peer),
        )
        copy.start()
        moves.append(copy)
    rows_ref[pl.ds(me * frame_dev, frame_dev)] = cot_ref[:, pl.ds(me * cells, cells)]
    total = mine[...]
    for k, copy in enumerate(stats):
        copy.wait_recv()
        total = total + theirs[k]
    stats_ref[...] = total

    @pl.when(me > 0)
    def _():
        up.wait_send()
        down.wait_recv()

    @pl.when(me < tiles - 1)
    def _():
        down.wait_send()
        up.wait_recv()

    for copy in stats:
        copy.wait_send()
    for copy in moves:
        copy.wait()


def exchange(video, top, bot, cot, tiles):
    frames, cells, channels = video.shape
    vmem = pl.BlockSpec(memory_space=pltpu.VMEM)
    dma = pltpu.SemaphoreType.DMA
    return pl.pallas_call(
        functools.partial(exchange_kernel, tiles),
        out_shape=[
            jax.ShapeDtypeStruct((2 * frames, 128), jnp.float32),
            jax.ShapeDtypeStruct((frames, cells, channels), jnp.bfloat16),
            jax.ShapeDtypeStruct(top.shape, jnp.bfloat16),
            jax.ShapeDtypeStruct(top.shape, jnp.bfloat16),
        ],
        in_specs=[vmem] * 4,
        out_specs=[vmem] * 4,
        scratch_shapes=[
            pltpu.VMEM((2 * frames, 128), jnp.float32),
            pltpu.VMEM((tiles - 1, 2 * frames, 128), jnp.float32),
            dma((tiles - 1,)),
            dma((tiles - 1,)),
            dma((2,)),
            dma((2,)),
            dma((tiles - 1,)),
            dma((tiles - 1,)),
        ],
        compiler_params=pltpu.CompilerParams(
            collective_id=0, has_side_effects=True, vmem_limit_bytes=32 << 20
        ),
    )(video, top, bot, cot)


def digits(dps, tiles):
    dp, tile = lax.axis_index("dp"), lax.axis_index("tile")
    return {
        "core": (2, lax.rem(dp, 2), lambda j: ((dp // 2) * 2 + j, tile)),
        "y": (dps // 2, dp // 2, lambda j: (j * 2 + lax.rem(dp, 2), tile)),
        "lo": (2, lax.rem(tile, 2), lambda j: (dp, (tile // 2) * 2 + j)),
        "hi": (tiles // 2, tile // 2, lambda j: (dp, j * 2 + lax.rem(tile, 2))),
    }


ORDERS = (("core", "lo", "y", "hi"), ("core", "y", "lo", "hi"))


def group_sizes(order, dps, tiles):
    known = {"core": 2, "y": dps // 2, "lo": 2, "hi": tiles // 2}
    return [known[name] for name in order]


def reduce_kernel(dps, tiles, enc_ref, grad_ref, out_ref, sum_ref, *scratch):
    chunks, pieces = grad_ref.shape[:2]
    scratch = list(scratch)
    enc_send, enc_recv, sends, recvs = scratch[-4:]
    bufs = scratch[:-4]
    dp, me = lax.axis_index("dp"), lax.axis_index("tile")
    frames, cells, _ = enc_ref.shape
    frame_dev = out_ref.shape[0]
    table = digits(dps, tiles)
    peers = [(dp, lax.rem(me + k, tiles)) for k in range(1, tiles)]
    greet = list(peers)
    for name in ("core", "y"):
        size, mine, peer = table[name]
        greet += [peer(lax.rem(mine + k, size)) for k in range(1, size)]
    barrier = pltpu.get_barrier_semaphore()
    for peer in greet:
        pl.semaphore_signal(barrier, inc=1, device_id=peer, device_id_type=MESH)
    pl.semaphore_wait(barrier, len(greet))

    used = [0]
    waiting = []

    def send(src, dst, peer):
        at = used[0]
        used[0] += 1
        copy = remote(src, dst, sends.at[at], recvs.at[at], peer)
        copy.start()
        waiting.append(copy)
        return copy

    stages = len(ORDERS[0])
    source = [grad_ref.at[c] for c in range(chunks)]
    base = [0] * chunks
    length = [pieces] * chunks
    offsets = [[] for _ in range(chunks)]
    pending = [None] * chunks
    moves = []

    def spread(c, s):
        size, mine, peer = table[ORDERS[c % 2][s]]
        part = length[c] // size
        slots = bufs[s * 2 * chunks + 2 * c]
        pending[c] = [
            send(
                source[c].at[pl.ds(lax.rem(mine + k, size) * part, part)],
                slots.at[k - 1],
                peer(lax.rem(mine + k, size)),
            )
            for k in range(1, size)
        ]

    def gather(c, s):
        size, mine, peer = table[ORDERS[c % 2][s]]
        start, count = offsets[c][s]
        pending[c] = [
            send(
                sum_ref.at[c, pl.ds(start, count)],
                sum_ref.at[c, pl.ds(start, count)],
                peer(lax.rem(mine + k, size)),
            )
            for k in range(1, size)
        ]

    for c in range(chunks):
        spread(c, 0)
    for k, peer in enumerate(peers):
        copy = remote(
            enc_ref.at[pl.ds(peer[1] * frame_dev, frame_dev)],
            out_ref.at[:, pl.ds(me * cells, cells)],
            enc_send.at[k],
            enc_recv.at[k],
            peer,
        )
        copy.start()
        moves.append(copy)
    out_ref[:, pl.ds(me * cells, cells)] = enc_ref[pl.ds(me * frame_dev, frame_dev)]
    for s in range(stages):
        for c in range(chunks):
            size, mine, _ = table[ORDERS[c % 2][s]]
            part = length[c] // size
            slots, total = bufs[s * 2 * chunks + 2 * c : s * 2 * chunks + 2 * c + 2]
            value = source[c][pl.ds(mine * part, part)].astype(jnp.float32)
            for k, copy in enumerate(pending[c]):
                copy.wait_recv()
                value = value + slots[k].astype(jnp.float32)
            base[c] = base[c] + mine * part
            offsets[c].append((base[c], part))
            length[c] = part
            if s + 1 < stages:
                total[...] = value.astype(jnp.bfloat16)
                source[c] = total
                spread(c, s + 1)
            else:
                sum_ref[c, pl.ds(base[c], part)] = value.astype(jnp.bfloat16)
                gather(c, s)
    for s in range(stages - 1, -1, -1):
        for c in range(chunks):
            for copy in pending[c]:
                copy.wait_recv()
            if s > 0:
                gather(c, s - 1)
    for copy in waiting:
        copy.wait_send()
    for copy in moves:
        copy.wait()


def reduce_all(enc, grads, dps, tiles):
    frames, cells, channels = enc.shape
    chunks, pieces, rows, width = grads.shape
    vmem = pl.BlockSpec(memory_space=pltpu.VMEM)
    dma = pltpu.SemaphoreType.DMA
    scratch = []
    copies = 0
    for s in range(4):
        for c in range(chunks):
            sizes = group_sizes(ORDERS[c % 2], dps, tiles)
            part = pieces // math.prod(sizes[: s + 1])
            scratch.append(pltpu.VMEM((sizes[s] - 1, part, rows, width), jnp.bfloat16))
            scratch.append(pltpu.VMEM((part, rows, width), jnp.bfloat16))
            copies += 2 * (sizes[s] - 1)
    scratch += [dma((tiles - 1,)), dma((tiles - 1,)), dma((copies,)), dma((copies,))]
    return pl.pallas_call(
        functools.partial(reduce_kernel, dps, tiles),
        out_shape=[
            jax.ShapeDtypeStruct((frames // tiles, cells * tiles, channels), jnp.bfloat16),
            jax.ShapeDtypeStruct(grads.shape, jnp.bfloat16),
        ],
        in_specs=[vmem] * 2,
        out_specs=[vmem] * 2,
        scratch_shapes=scratch,
        compiler_params=pltpu.CompilerParams(
            collective_id=1, has_side_effects=True, vmem_limit_bytes=32 << 20
        ),
    )(enc, grads)


def contract_rows(left, right):
    return lax.dot_general(
        left, right, (((0,), (0,)), ((), ())), preferred_element_type=jnp.float32
    )


def patch_columns(padded, strip_rows, frame_width):
    pieces = [
        padded[:, i : i + strip_rows, j : j + frame_width, :]
        for i in range(3)
        for j in range(3)
    ]
    return jnp.concatenate(pieces, axis=-1).reshape(-1, 9 * padded.shape[-1])


def on_device(
    video_in, clip_lengths, norm_gain, norm_bias, spatial_weight, temporal_weight, cotangent
):
    dps, tiles = lax.axis_size("dp"), lax.axis_size("tile")
    _, frames, strip, width, channels = video_in.shape
    height = strip * tiles
    cells = strip * width
    frame_dev = frames // tiles
    tile = lax.axis_index("tile")
    video = video_in[0]
    top = video[:, 0].reshape(frames * width, channels)
    bot = video[:, strip - 1].reshape(frames * width, channels)
    stats, cot, above, below = exchange(
        video.reshape(frames, cells, channels),
        top,
        bot,
        cotangent[0].reshape(frame_dev, height * width, channels),
        tiles,
    )
    lengths = clip_lengths[0]
    clips = lengths.shape[0]
    upto = jnp.arange(clips)[:, None] >= jnp.arange(clips)[None, :]
    ends = jnp.sum(jnp.where(upto, lengths[None, :], 0), axis=1)
    ids = jnp.arange(frames, dtype=jnp.int32)
    clip_of = jnp.sum((ids[:, None] >= ends[None, :]).astype(jnp.int32), axis=1)
    same = clip_of[:, None] == clip_of[None, :]
    position = jnp.sum((same & (ids[None, :] < ids[:, None])).astype(jnp.int32), axis=1)
    member = same.astype(jnp.float32)
    per_group = channels // GROUPS
    count = jnp.sum(member, axis=1) * (height * width * per_group)

    def over_clip(part):
        return jnp.dot(member, part, precision=lax.Precision.HIGHEST) / count[:, None]

    mean = over_clip(stats[:frames, :GROUPS])
    var = jnp.maximum(over_clip(stats[frames:, :GROUPS]) - mean * mean, 0.0)
    mean_c = jnp.repeat(mean, per_group, axis=1)[:, None, None, :]
    rstd_c = jnp.repeat(lax.rsqrt(var + norm_eps), per_group, axis=1)[:, None, None, :]
    local_vals = video.astype(jnp.float32)
    halo = (frames, 1, width, channels)
    wide = jnp.concatenate([above.reshape(halo), video, below.reshape(halo)], axis=1)
    normed = (wide.astype(jnp.float32) - mean_c) * rstd_c * norm_gain + norm_bias
    row = jnp.arange(strip + 2) + tile * strip - 1
    inside = ((row >= 0) & (row < height))[None, :, None, None]
    active = jnp.where(inside, jax.nn.silu(normed), 0.0).astype(jnp.bfloat16)
    padded = jnp.pad(active, ((0, 0), (0, 0), (1, 1), (0, 0)))
    columns = patch_columns(padded, strip, width)
    conv_out = jnp.dot(
        columns, spatial_weight.reshape(9 * channels, channels), preferred_element_type=jnp.float32
    )
    block_out = (local_vals + conv_out.reshape(local_vals.shape)).astype(jnp.bfloat16)
    block_out = block_out.reshape(frames, cells, channels)

    earlier = []
    later = []
    for k in range(3):
        moved = jnp.pad(block_out, ((k, 0), (0, 0), (0, 0)))[:frames]
        earlier.append(jnp.where((position >= k)[:, None, None], moved, jnp.zeros_like(moved)))
        moved = jnp.pad(cot, ((0, k), (0, 0), (0, 0)))[k:]
        ahead = jnp.pad(position, (0, k))[k:]
        later.append(jnp.where((ahead >= k)[:, None, None], moved, jnp.zeros_like(moved)))
    earlier = jnp.concatenate(earlier, axis=-1).reshape(-1, 3 * channels)
    later = jnp.concatenate(later, axis=-1).reshape(-1, 3 * channels)
    lifted = jnp.dot(
        earlier, temporal_weight.reshape(3 * channels, channels), preferred_element_type=jnp.float32
    ).reshape(block_out.shape)
    encoded = (block_out.astype(jnp.float32) + lifted).astype(jnp.bfloat16)
    back_weight = jnp.transpose(temporal_weight, (0, 2, 1)).reshape(3 * channels, channels)
    pulled = jnp.dot(later, back_weight, preferred_element_type=jnp.float32).reshape(cot.shape)
    grad_block = (cot.astype(jnp.float32) + pulled).astype(jnp.bfloat16)
    temporal_term = contract_rows(earlier, cot.reshape(-1, channels))
    spatial_term = contract_rows(columns, grad_block.reshape(-1, channels))
    grads = jnp.concatenate([spatial_term, temporal_term], axis=0).astype(jnp.bfloat16)
    chunks = 6
    pieces = dps * tiles
    out, total = reduce_all(
        encoded,
        grads.reshape(chunks, pieces, 12 * channels // (chunks * pieces), channels),
        dps,
        tiles,
    )
    scale = 1.0 / math.sqrt(dps * frames * height * width)
    total = total.reshape(12, channels, channels).astype(jnp.float32) * scale
    return (
        out.reshape(1, frame_dev, height, width, channels),
        total[:9].reshape(3, 3, channels, channels),
        total[9:],
    )


def solution(mesh):
    return jax.shard_map(
        on_device,
        mesh=mesh,
        in_specs=(
            P("dp", None, "tile", None, None),
            P("dp", None),
            P(),
            P(),
            P(),
            P(),
            P("dp", "tile", None, None, None),
        ),
        out_specs=(P("dp", "tile", None, None, None), P(), P()),
        check_vma=False,
    )
```

time: 226 us -> 65.6 us (0.29)
  waiting for transfers between devices: 153 us -> 0 us
  Pallas kernels: 0 us -> 49.2 us
  blocking collectives: 19 us -> 0 us
  starting transfers between devices: 14 us -> 0 us
  between operations: 14.4 us -> 0.85 us
  matrix products: 9.43 us -> 3.19 us
  other arithmetic: 6.79 us -> 3.31 us
    psum x1 -> x0, waiting for transfers between devices: 141 us -> none  [on_device(): lax.psum((spatial_term * grad_scale, temporal_term * grad_scale), ('dp',...]
    pallas_call x0 -> x2, Pallas kernels: none -> 49.2 us  [the longest x1 35.4 us: reduce_all(): pl.pallas_call(functools.partial(reduce_kernel, dps, tiles), out_shape=[j...]
    psum x1 -> x0, blocking collectives: 19 us -> none  [on_device(): lax.psum((group_total(onehot, frame_sum, GROUPS), group_total(onehot, jnp...]
    all_to_all x2 -> x0, waiting for transfers between devices: 9.12 us -> none  [the longest x1 5.5 us: on_device(): lax.all_to_all(block_out[None], 'tile', split_axis=1, concat_axis=2, tile...]
    ppermute x4 -> x0, starting transfers between devices: 7.11 us -> none  [the longest x2 4.52 us: from_behind(): return lax.ppermute(shard, axis, pairs)]
    all_to_all x2 -> x0, starting transfers between devices: 6.83 us -> none  [the longest x1 3.41 us: on_device(): lax.all_to_all(grad_time[None], 'tile', split_axis=2, concat_axis=1, tile...]
    dot_general x2, matrix products: 5.18 us -> 1.25 us  [contract_rows(): lax.dot_general(left, right, (((0,), (0,)), ((), ())), preferred_element_...]
    slice x1 -> x2, local copies, waits for them, and re-layouts: 0.01 us -> 2.49 us  [the longest x1 1.56 us: on_device(): total[:9].reshape(3, 3, channels, channels)]
  transfers between devices with their start and end apart: 7 -> 0, of which waited for: 4 -> 0; matrix products, arithmetic and copies ran while one was open for 4% -> 0% of each run, Pallas kernels for 0% -> 0%
where the time goes in v1:
time: 65.6 us; the launch traced here: 65.2 us
  Pallas kernels  49.2 us (75%)
  local copies, waits for them, and re-layouts  8.65 us (13%)
  other arithmetic  3.31 us (5%)
  matrix products  3.19 us (5%)
  between operations  0.85 us (1%)
    pallas_call x1, Pallas kernels, reduce_all(): pl.pallas_call(functools.partial(reduce_kernel, dps, tiles), out_shape=[j...  35.4 us
    pallas_call x1, Pallas kernels, exchange(): pl.pallas_call(functools.partial(exchange_kernel, tiles), out_shape=[jax....  13.9 us
    unnamed x20, local copies, waits for them, and re-layouts  4.91 us
    slice x1, local copies, waits for them, and re-layouts, on_device(): total[:9].reshape(3, 3, channels, channels)  1.56 us

profile of v1, /device:TPU:1, one launch (start us, length us, event | category | flops | bytes accessed | tf_op | source)
XLA Modules:
  0.0 65.2 jit_solution(2427687522104456424)
XLA Ops:
  0.7 1.2 %copy-done = bf16[3,3,256,256]{3,2,1,0:T(8,128)(2,1)S(1)} copy-done((bf16[3,3,256,256]{3,2,1,0:T(8,128)(2,1)S(1)}, bf16[3,3,256,256]{3,2,1,0:T(8,128)(2,1)}, u32[]{:S(2)}) %copy-start) | copy-done | bytes 1179672
  1.9 0.8 %select_reduce_fusion = s32[6]{0:T(128)S(1)} fusion(s32[6]{0:T(128)} %bitcast.66), kind=kLoop, calls=%fused_computation.66 | loop fusion | flops 102 | bytes 48 | tf_op jit(solution)/shard_map/reduce_sum | solution.py:338
  2.7 0.1 convert_reduce_fusion.1
  2.8 0.2 fusion.26
  3.0 0.2 convert_reduce_fusion
  3.1 0.1 slice_compare_fusion.1
  3.2 0.9 %slice_bitcast_fusion = (bf16[128,256]{1,0:T(8,128)(2,1)S(1)}, bf16[128,256]{1,0:T(8,128)(2,1)S(1)}) fusion(bf16[16,4,8,256]{3,2,1,0:T(8,128)(2,1)} %bitcast.53), kind=kLoop, calls=%fused_computation.50 | loop fusion | bytes 262144 | tf_op jit(solution)/shard_map/reshape;squeeze | solution.py:327
  4.1 0.9 %copy-done.1 = bf16[1,16,4,8,256]{4,3,2,1,0:T(8,128)(2,1)S(1)} copy-done((bf16[1,16,4,8,256]{4,3,2,1,0:T(8,128)(2,1)S(1)}, bf16[1,16,4,8,256]{4,3,2,1,0:T(8,128)(2,1)}, u32[]{:S(2)}) %copy-start.1) | copy-done | bytes 262168
  5.1 0.9 %copy-done.3 = bf16[1,2,32,8,256]{4,3,2,1,0:T(8,128)(2,1)S(1)} copy-done((bf16[1,2,32,8,256]{4,3,2,1,0:T(8,128)(2,1)S(1)}, bf16[1,2,32,8,256]{4,3,2,1,0:T(8,128)(2,1)}, u32[]{:S(2)}) %copy-start.3) | copy-done | bytes 262168
  6.0 13.9 %shard_map.94 = (f32[32,128]{1,0:T(8,128)S(1)}, bf16[16,32,256]{2,1,0:T(8,128)(2,1)S(1)}, bf16[128,256]{1,0:T(8,128)(2,1)S(1)}, bf16[128,256]{1,0:T(8,128)(2,1)S(1)}) custom-call(bf16[16,32,256]{2,1,0:T(8,128)(2,1)S(1)} %bitcast.55, bf16[128,256]{1,0:T(8,128)(2,1)S(1)} %get-tuple-element.22.top_ref, bf16[128,256]{1,0:T(8,128)(2,1)S(1)} %get-tuple-element.21.bot_ref, ...), custom_call_target="tpu_custom_call" | custom-call | tf_op jit(solution)/shard_map/pallas_call | solution.py:120
  19.9 0.2 convolution_divide_fusion.1
  20.1 0.2 fusion.8
  20.3 0.1 copy.21
  20.4 0.1 copy.23
  20.6 1.3 %select_convert_fusion = bf16[16,6,8,256]{3,2,1,0:T(8,128)(2,1)S(1)} fusion(bf16[16,1,8,256]{3,2,1,0:T(8,128)(2,1)S(1)} %bitcast.59, bf16[16,4,8,256]{3,2,1,0:T(8,128)(2,1)} %bitcast.54, bf16[16,1,8,256]{3,2,1,0:T(8,128)(2,1)S(1)} %bitcast.58, f32[256]{0:T(256)} %param.10, f32[256]{0:T(256)} %param.9, f32[16,256]{1,0:T(8,128)S(1)} %copy.24, ...), kind=kLoop, calls=%fused_computation.30 | loop fusion | flops 2555904 | bytes 821254 | tf_op jit(solution)/shard_map/convert_element_type | solution.py:360
  21.9 0.2 copy.25
  22.1 0.1 fusion.18
  22.3 0.1 fusion.20
  22.4 0.1 fusion.21
  22.6 0.5 copy-done.2
  23.1 0.8 %fusion.4 = bf16[16,32,256]{2,1,0:T(8,128)(2,1)S(1)} fusion(bf16[16,4,8,2304]{3,2,1,0:T(8,128)(2,1)S(1)} %fusion.23, bf16[2304,256,1,1]{1,0,3,2:T(8,128)(2,1)S(1)} %bitcast.51, bf16[1,16,4,8,256]{4,3,2,1,0:T(8,128)(2,1)S(1)} %copy-done.2), kind=kOutput, calls=%fused_computation.17 | convolution fusion | flops 604372992 | bytes 4063232 | tf_op jit(solution)/shard_map/dot_general | solution.py:363
  23.9 0.2 broadcast_select_fusion
  24.1 0.4 fusion.2.enc_ref
  24.5 0.4 fusion.3
  24.9 0.4 fusion
  25.3 0.8 %convolution_convert_fusion = bf16[2304,256]{1,0:T(8,128)(2,1)S(1)} fusion(bf16[512,2304]{1,0:T(8,128)(2,1)S(1)} %bitcast.65, bf16[512,256]{1,0:T(8,128)(2,1)S(1)} %bitcast.67), kind=kOutput, calls=%fused_computation | convolution fusion | flops 604569600 | bytes 3801088 | tf_op jit(solution)/shard_map/dot_general | solution.py:302
  26.1 0.1 pad_maximum_fusion
  26.2 35.4 %shard_map.95 = (bf16[2,256,256]{2,1,0:T(8,128)(2,1)S(1)}, bf16[6,32,16,256]{3,2,1,0:T(8,128)(2,1)S(1)}) custom-call(bf16[16,32,256]{2,1,0:T(8,128)(2,1)S(1)} %fusion.2.enc_ref, bf16[6,32,16,256]{3,2,1,0:T(8,128)(2,1)S(1)} %bitcast.52), custom_call_target="tpu_custom_call" | custom-call | tf_op jit(solution)/shard_map/pallas_call | solution.py:286
  61.6 0.4 convert_multiply_fusion
  62.0 0.9 %slice.93 = f32[3,256,256]{2,1,0:T(8,128)} slice(f32[12,256,256]{2,1,0:T(8,128)S(1)} %bitcast.60), slice={[9:12], [0:256], [0:256]} | slice | bytes 1572864 | tf_op jit(solution)/shard_map/slice | solution.py:402
  63.0 1.6 %slice.92 = f32[9,256,256]{2,1,0:T(8,128)} slice(f32[12,256,256]{2,1,0:T(8,128)S(1)} %bitcast.61), slice={[0:9], [0:256], [0:256]} | slice | bytes 4718592 | tf_op jit(solution)/shard_map/slice | solution.py:401
  64.5 0.7 %copy.36 = bf16[1,2,32,8,256]{4,3,2,1,0:T(8,128)(2,1)} copy(bf16[1,2,32,8,256]{4,3,2,1,0:T(8,128)(2,1)S(1)} %bitcast.57) | data formatting | bytes 524288
  (18 shorter events, 0.4 us)
Async XLA Ops:
  0.6 1.3 %copy-start = (bf16[3,3,256,256]{3,2,1,0:T(8,128)(2,1)S(1)}, bf16[3,3,256,256]{3,2,1,0:T(8,128)(2,1)}, u32[]{:S(2)}) copy-start(bf16[3,3,256,256]{3,2,1,0:T(8,128)(2,1)} %param.11) | copy-start | bytes 3538948
  4.1 1.0 %copy-start.1 = (bf16[1,16,4,8,256]{4,3,2,1,0:T(8,128)(2,1)S(1)}, bf16[1,16,4,8,256]{4,3,2,1,0:T(8,128)(2,1)}, u32[]{:S(2)}) copy-start(bf16[1,16,4,8,256]{4,3,2,1,0:T(8,128)(2,1)} %param.7) | copy-start | bytes 786436
  5.1 0.9 %copy-start.3 = (bf16[1,2,32,8,256]{4,3,2,1,0:T(8,128)(2,1)S(1)}, bf16[1,2,32,8,256]{4,3,2,1,0:T(8,128)(2,1)}, u32[]{:S(2)}) copy-start(bf16[1,2,32,8,256]{4,3,2,1,0:T(8,128)(2,1)} %param.13) | copy-start | bytes 786436
  6.0 15.9 %copy-start.4 = (bf16[3,256,256]{2,1,0:T(8,128)(2,1)S(1)}, bf16[3,256,256]{2,1,0:T(8,128)(2,1)}, u32[]{:S(2)}) copy-start(bf16[3,256,256]{2,1,0:T(8,128)(2,1)} %param.12) | copy-start | bytes 1179652
  22.2 1.0 %copy-start.2 = (bf16[1,16,4,8,256]{4,3,2,1,0:T(8,128)(2,1)S(1)}, bf16[1,16,4,8,256]{4,3,2,1,0:T(8,128)(2,1)}, u32[]{:S(2)}) copy-start(bf16[1,16,4,8,256]{4,3,2,1,0:T(8,128)(2,1)} %param.7) | copy-start | bytes 786436

commit v2 on v0

v2 whole, which is shorter than its diff:
```python
import functools
import math

import jax
import jax.numpy as jnp
from jax import lax
from jax.experimental import pallas as pl
from jax.experimental.pallas import tpu as pltpu
from jax.sharding import PartitionSpec as P

GROUPS = 32
MESH = pl.DeviceIdType.MESH
norm_eps = 1e-05


def remote(src, dst, send, recv, peer):
    return pltpu.make_async_remote_copy(
        src_ref=src,
        dst_ref=dst,
        send_sem=send,
        recv_sem=recv,
        device_id=peer,
        device_id_type=MESH,
    )


def digits(dps, tiles):
    dp, tile = lax.axis_index("dp"), lax.axis_index("tile")
    return {
        "core": (2, lax.rem(dp, 2), lambda j: ((dp // 2) * 2 + j, tile)),
        "y": (dps // 2, dp // 2, lambda j: (j * 2 + lax.rem(dp, 2), tile)),
        "lo": (2, lax.rem(tile, 2), lambda j: (dp, (tile // 2) * 2 + j)),
        "hi": (tiles // 2, tile // 2, lambda j: (dp, j * 2 + lax.rem(tile, 2))),
    }


ORDERS = (("core", "lo", "y", "hi"), ("core", "y", "lo", "hi"))


def group_sizes(order, dps, tiles):
    known = {"core": 2, "y": dps // 2, "lo": 2, "hi": tiles // 2}
    return [known[name] for name in order]


def pick_rows(lengths_ref, frame):
    clip, end = jnp.zeros_like(frame), 0
    for c in range(lengths_ref.shape[1]):
        end = end + lengths_ref[0, c]
        clip = clip + jnp.where(frame >= end, 1, 0)
    return clip


def dot32(a, b):
    return jnp.dot(
        a, b, precision=lax.Precision.HIGHEST, preferred_element_type=jnp.float32
    )


def contract(a, b, da, db):
    return lax.dot_general(
        a, b, (((da,), (db,)), ((), ())), preferred_element_type=jnp.float32
    )


def block_kernel(
    dps,
    tiles,
    width,
    lengths_ref,
    video_ref,
    strips_ref,
    cot_ref,
    gain_ref,
    bias_ref,
    sw_ref,
    tw_ref,
    out_ref,
    sum_ref,
    *scratch,
):
    scratch = list(scratch)
    mine, theirs, above, below, cot_rows, cols, early, late = scratch[:8]
    stat_send, stat_recv, halo_send, halo_recv, cot_send, cot_recv = scratch[8:14]
    enc_send, enc_recv, sends, recvs = scratch[14:18]
    bufs = scratch[18:]
    dp, me = lax.axis_index("dp"), lax.axis_index("tile")
    frames, cells, channels = video_ref.shape
    strip = cells // width
    height = strip * tiles
    rows = frames * cells
    frame_dev = cot_ref.shape[0]
    chunks, pieces = sum_ref.shape[:2]
    bf16, f32 = jnp.bfloat16, jnp.float32
    table = digits(dps, tiles)
    peers = [(dp, lax.rem(me + k, tiles)) for k in range(1, tiles)]
    greet = list(peers)
    for name in ("core", "y"):
        size, at, peer = table[name]
        greet += [peer(lax.rem(at + k, size)) for k in range(1, size)]
    barrier = pltpu.get_barrier_semaphore()
    for peer in greet:
        pl.semaphore_signal(barrier, inc=1, device_id=peer, device_id_type=MESH)

    values = video_ref[...].astype(f32)
    sums = jnp.concatenate(
        [jnp.sum(values, axis=1), jnp.sum(values * values, axis=1)], axis=0
    )
    lanes = mine.shape[1]
    per_group = channels // GROUPS
    member = lax.broadcasted_iota(jnp.int32, (channels, lanes), 0) // per_group
    group = lax.broadcasted_iota(jnp.int32, (channels, lanes), 1)
    mine[...] = dot32(sums, jnp.where(member == group, 1.0, 0.0).astype(f32))
    pl.semaphore_wait(barrier, len(greet))

    stats = []
    for k, peer in enumerate(peers):
        copy = remote(mine, theirs.at[k], stat_send.at[k], stat_recv.at[k], peer)
        copy.start()
        stats.append(copy)
    up = remote(strips_ref.at[:, 0], below, halo_send.at[0], halo_recv.at[0], (dp, me - 1))
    down = remote(
        strips_ref.at[:, strip - 1], above, halo_send.at[1], halo_recv.at[1], (dp, me + 1)
    )

    @pl.when(me > 0)
    def _():
        up.start()

    @pl.when(me < tiles - 1)
    def _():
        down.start()

    moves = []
    for k, peer in enumerate(peers):
        copy = remote(
            cot_ref.at[:, pl.ds(peer[1] * cells, cells)],
            cot_rows.at[pl.ds(me * frame_dev, frame_dev)],
            cot_send.at[k],
            cot_recv.at[k],
            peer,
        )
        copy.start()
        moves.append(copy)
    cot_rows[pl.ds(me * frame_dev, frame_dev)] = cot_ref[:, pl.ds(me * cells, cells)]

    clip_a = pick_rows(lengths_ref, lax.broadcasted_iota(jnp.int32, (frames, frames), 0))
    clip_b = pick_rows(lengths_ref, lax.broadcasted_iota(jnp.int32, (frames, frames), 1))
    same = jnp.where(clip_a == clip_b, 1.0, 0.0).astype(f32)
    count = jnp.sum(same, axis=1, keepdims=True) * (height * width * per_group)
    frame = lax.broadcasted_iota(jnp.int32, (rows, 1), 0) // cells
    clip = pick_rows(lengths_ref, frame)
    keeps = [None] + [
        jnp.where(
            jnp.logical_and(clip == pick_rows(lengths_ref, frame - k), frame >= k), 1.0, 0.0
        ).astype(f32)
        for k in (1, 2)
    ]
    member = lax.broadcasted_iota(jnp.int32, (lanes, channels), 1) // per_group
    group = lax.broadcasted_iota(jnp.int32, (lanes, channels), 0)
    widen = jnp.where(member == group, 1.0, 0.0).astype(f32)
    total = mine[...]
    for k, copy in enumerate(stats):
        copy.wait_recv()
        total = total + theirs[k]
    mean = dot32(same, total[:frames]) / count
    var = jnp.maximum(dot32(same, total[frames:]) / count - mean * mean, 0.0)
    mean = dot32(mean, widen)
    slope = dot32(lax.rsqrt(var + norm_eps), widen) * gain_ref[...]
    bias = bias_ref[...]

    @pl.when(me > 0)
    def _():
        down.wait_recv()

    @pl.when(me < tiles - 1)
    def _():
        up.wait_recv()

    ext = cells + 2 * width
    line = lax.broadcasted_iota(jnp.int32, (ext, channels), 0)
    row = line // width + me * strip - 1
    inside = jnp.logical_and(row >= 0, row < height)
    col = lax.rem(line, width)
    for f in range(frames):
        v = jnp.concatenate(
            [above[f].astype(f32), video_ref[f].astype(f32), below[f].astype(f32)], axis=0
        )
        v = (v - mean[f : f + 1]) * slope[f : f + 1] + bias
        v = jnp.where(inside, v / (1.0 + jnp.exp(-v)), 0.0)
        shifted = (
            jnp.where(col == 0, 0.0, pltpu.roll(v, 1, 0)),
            v,
            jnp.where(col == width - 1, 0.0, pltpu.roll(v, ext - 1, 0)),
        )
        for i in range(3):
            for j in range(3):
                tap = (i * 3 + j) * channels
                cols[f * cells : (f + 1) * cells, tap : tap + channels] = shifted[j][
                    i * width : i * width + cells
                ].astype(bf16)
    conv = jnp.dot(cols[...], sw_ref[...], preferred_element_type=f32)
    block = video_ref[...].astype(f32).reshape(rows, channels) + conv
    block = block.astype(bf16)
    early[:, :channels] = block
    block = block.astype(f32)
    for k in (1, 2):
        lag = k * cells
        span = slice(k * channels, (k + 1) * channels)
        early[:lag, span] = jnp.zeros((lag, channels), bf16)
        early[lag:, span] = (block[: rows - lag] * keeps[k][lag:]).astype(bf16)
    lifted = jnp.dot(early[...], tw_ref[...], preferred_element_type=f32)
    enc = bufs[0]
    enc[...] = (block + lifted).astype(bf16).reshape(frames, cells, channels)
    for k, peer in enumerate(peers):
        copy = remote(
            enc.at[pl.ds(peer[1] * frame_dev, frame_dev)],
            out_ref.at[:, pl.ds(me * cells, cells)],
            enc_send.at[k],
            enc_recv.at[k],
            peer,
        )
        copy.start()
        moves.append(copy)
    out_ref[:, pl.ds(me * cells, cells)] = enc[pl.ds(me * frame_dev, frame_dev)]

    for copy in moves[: tiles - 1]:
        copy.wait_recv()
    cot = cot_rows[...].reshape(rows, channels)
    cot32 = cot.astype(f32)
    late[:, :channels] = cot
    for k in (1, 2):
        lag = k * cells
        span = slice(k * channels, (k + 1) * channels)
        late[: rows - lag, span] = (cot32[lag:] * keeps[k][lag:]).astype(bf16)
        late[rows - lag :, span] = jnp.zeros((lag, channels), bf16)
    grad_block = cot32
    for k in range(3):
        span = slice(k * channels, (k + 1) * channels)
        grad_block = grad_block + contract(late[:, span], tw_ref[span, :], 1, 1)
    grad_block = grad_block.astype(bf16)

    sent = [0]
    waiting = []

    def send(src, dst, peer):
        at = sent[0]
        sent[0] += 1
        copy = remote(src, dst, sends.at[at], recvs.at[at], peer)
        copy.start()
        waiting.append(copy)
        return copy

    stages = len(ORDERS[0])
    narrow = bufs[1 : 1 + chunks]
    exact = bufs[1 + chunks : 1 + 2 * chunks]
    bufs = bufs[1 + 2 * chunks :]
    base = [0] * chunks
    length = [pieces] * chunks
    offsets = [[] for _ in range(chunks)]
    pending = [None] * chunks

    def spread(c, s):
        size, at, peer = table[ORDERS[c % 2][s]]
        part = length[c] // size
        slots = bufs[3 * (s * chunks + c)]
        pending[c] = [
            send(
                narrow[c].at[pl.ds(lax.rem(at + k, size) * part, part)],
                slots.at[k - 1],
                peer(lax.rem(at + k, size)),
            )
            for k in range(1, size)
        ]

    def gather(c, s):
        size, at, peer = table[ORDERS[c % 2][s]]
        start, number = offsets[c][s]
        here = sum_ref.at[c, pl.ds(start, number)]
        pending[c] = [
            send(here, here, peer(lax.rem(at + k, size))) for k in range(1, size)
        ]

    taps = 12 // chunks
    for c in range(chunks):
        parts = []
        for tap in range(c * taps, (c + 1) * taps):
            if tap < 9:
                left, right = cols[:, tap * channels : (tap + 1) * channels], grad_block
            else:
                left, right = early[:, (tap - 9) * channels : (tap - 8) * channels], cot
            parts.append(contract(left, right, 0, 0))
        value = jnp.concatenate(parts, axis=0).reshape(exact[c].shape)
        exact[c][...] = value
        narrow[c][...] = value.astype(bf16)
        spread(c, 0)
    for s in range(stages):
        for c in range(chunks):
            size, at, _ = table[ORDERS[c % 2][s]]
            part = length[c] // size
            slots, total16, total32 = bufs[3 * (s * chunks + c) : 3 * (s * chunks + c) + 3]
            value = exact[c][pl.ds(at * part, part)]
            for k, copy in enumerate(pending[c]):
                copy.wait_recv()
                value = value + slots[k].astype(f32)
            base[c] = base[c] + at * part
            offsets[c].append((base[c], part))
            length[c] = part
            if s + 1 < stages:
                total16[...] = value.astype(bf16)
                total32[...] = value
                narrow[c], exact[c] = total16, total32
                spread(c, s + 1)
            else:
                sum_ref[c, pl.ds(base[c], part)] = value.astype(bf16)
                gather(c, s)
    for s in range(stages - 1, -1, -1):
        for c in range(chunks):
            for copy in pending[c]:
                copy.wait_recv()
            if s > 0:
                gather(c, s - 1)

    @pl.when(me > 0)
    def _():
        up.wait_send()

    @pl.when(me < tiles - 1)
    def _():
        down.wait_send()

    for copy in stats[: tiles - 1] + moves + waiting:
        copy.wait_send()
    for copy in moves[tiles - 1 :]:
        copy.wait_recv()


def residual_block(lengths, video, strips, cot, gain, bias, sw, tw, dps, tiles, chunks):
    frames, cells, channels = video.shape
    width = strips.shape[2]
    pieces = dps * tiles
    depth = 12 * channels // (chunks * pieces)
    rows = frames * cells
    bf16, f32 = jnp.bfloat16, jnp.float32
    vmem = pl.BlockSpec(memory_space=pltpu.VMEM)
    dma = pltpu.SemaphoreType.DMA
    bufs = [pltpu.VMEM((frames, cells, channels), bf16)]
    bufs += [pltpu.VMEM((pieces, depth, channels), bf16)] * chunks
    bufs += [pltpu.VMEM((pieces, depth, channels), f32)] * chunks
    copies = 0
    for s in range(len(ORDERS[0])):
        for c in range(chunks):
            sizes = group_sizes(ORDERS[c % 2], dps, tiles)
            part = pieces // math.prod(sizes[: s + 1])
            bufs.append(pltpu.VMEM((sizes[s] - 1, part, depth, channels), bf16))
            bufs.append(pltpu.VMEM((part, depth, channels), bf16))
            bufs.append(pltpu.VMEM((part, depth, channels), f32))
            copies += 2 * (sizes[s] - 1)
    halo = pltpu.VMEM((frames, width, channels), bf16)
    scratch = [
        pltpu.VMEM((2 * frames, 128), f32),
        pltpu.VMEM((tiles - 1, 2 * frames, 128), f32),
        halo,
        halo,
        pltpu.VMEM((frames, cells, channels), bf16),
        pltpu.VMEM((rows, 9 * channels), bf16),
        pltpu.VMEM((rows, 3 * channels), bf16),
        pltpu.VMEM((rows, 3 * channels), bf16),
        dma((tiles - 1,)),
        dma((tiles - 1,)),
        dma((2,)),
        dma((2,)),
        dma((tiles - 1,)),
        dma((tiles - 1,)),
        dma((tiles - 1,)),
        dma((tiles - 1,)),
        dma((copies,)),
        dma((copies,)),
    ]
    return pl.pallas_call(
        functools.partial(block_kernel, dps, tiles, width),
        out_shape=[
            jax.ShapeDtypeStruct((frames // tiles, cells * tiles, channels), bf16),
            jax.ShapeDtypeStruct((chunks, pieces, depth, channels), bf16),
        ],
        in_specs=[
            pl.BlockSpec(memory_space=pltpu.SMEM),
            vmem,
            pl.BlockSpec(memory_space=pl.ANY),
            vmem,
            vmem,
            vmem,
            vmem,
            vmem,
        ],
        out_specs=[vmem] * 2,
        scratch_shapes=scratch + bufs,
        compiler_params=pltpu.CompilerParams(
            collective_id=0, has_side_effects=True, vmem_limit_bytes=48 << 20
        ),
    )(lengths, video, strips, cot, gain, bias, sw, tw)


def on_device(
    video_in, clip_lengths, norm_gain, norm_bias, spatial_weight, temporal_weight, cotangent
):
    dps, tiles = lax.axis_size("dp"), lax.axis_size("tile")
    _, frames, strip, width, channels = video_in.shape
    height = strip * tiles
    frame_dev = frames // tiles
    out, total = residual_block(
        clip_lengths,
        video_in[0].reshape(frames, strip * width, channels),
        video_in[0],
        cotangent[0].reshape(frame_dev, height * width, channels),
        norm_gain[None],
        norm_bias[None],
        spatial_weight.reshape(9 * channels, channels),
        temporal_weight.reshape(3 * channels, channels),
        dps,
        tiles,
        6,
    )
    scale = 1.0 / math.sqrt(dps * frames * height * width)
    total = total.reshape(12 * channels, channels)
    spatial, temporal = lax.optimization_barrier(
        (total[: 9 * channels], total[9 * channels :])
    )
    return (
        out.reshape(1, frame_dev, height, width, channels),
        (spatial.astype(jnp.float32) * scale).reshape(3, 3, channels, channels),
        (temporal.astype(jnp.float32) * scale).reshape(3, channels, channels),
    )


def solution(mesh):
    return jax.shard_map(
        on_device,
        mesh=mesh,
        in_specs=(
            P("dp", None, "tile", None, None),
            P("dp", None),
            P(),
            P(),
            P(),
            P(),
            P("dp", "tile", None, None, None),
        ),
        out_specs=(P("dp", "tile", None, None, None), P(), P()),
        check_vma=False,
    )
```

time: 226 us -> 60.5 us (0.27)
  waiting for transfers between devices: 153 us -> 0 us
  Pallas kernels: 0 us -> 50 us
  blocking collectives: 19 us -> 0 us
  starting transfers between devices: 14 us -> 0 us
  between operations: 14.4 us -> 0.67 us
  matrix products: 9.43 us -> 0 us
  other arithmetic: 6.79 us -> 2.49 us
    psum x1 -> x0, waiting for transfers between devices: 141 us -> none  [on_device(): lax.psum((spatial_term * grad_scale, temporal_term * grad_scale), ('dp',...]
    pallas_call x0 -> x1, Pallas kernels: none -> 50 us  [residual_block(): pl.pallas_call(functools.partial(block_kernel, dps, tiles, width), out_sh...]
    psum x1 -> x0, blocking collectives: 19 us -> none  [on_device(): lax.psum((group_total(onehot, frame_sum, GROUPS), group_total(onehot, jnp...]
    dot_general x9 -> x0, matrix products: 9.43 us -> none  [the longest x2 5.18 us: contract_rows(): lax.dot_general(left, right, (((0,), (0,)), ((), ())), preferred_element_...]
    all_to_all x2 -> x0, waiting for transfers between devices: 9.12 us -> none  [the longest x1 5.5 us: on_device(): lax.all_to_all(block_out[None], 'tile', split_axis=1, concat_axis=2, tile...]
    ppermute x4 -> x0, starting transfers between devices: 7.11 us -> none  [the longest x2 4.52 us: from_behind(): return lax.ppermute(shard, axis, pairs)]
    all_to_all x2 -> x0, starting transfers between devices: 6.83 us -> none  [the longest x1 3.41 us: on_device(): lax.all_to_all(grad_time[None], 'tile', split_axis=2, concat_axis=1, tile...]
    unnamed x24 -> x15, local copies, waits for them, and re-layouts: 6 us -> 6.87 us
  transfers between devices with their start and end apart: 7 -> 0, of which waited for: 4 -> 0; matrix products, arithmetic and copies ran while one was open for 4% -> 0% of each run, Pallas kernels for 0% -> 0%
where the time goes in v2:
time: 60.5 us; the launch traced here: 60.2 us
  Pallas kernels  50 us (83%)
  local copies, waits for them, and re-layouts  6.98 us (12%)
  other arithmetic  2.49 us (4%)
  between operations  0.67 us (1%)
    pallas_call x1, Pallas kernels, residual_block(): pl.pallas_call(functools.partial(block_kernel, dps, tiles, width), out_sh...  50 us
    unnamed x15, local copies, waits for them, and re-layouts  6.87 us
    mul x1, other arithmetic, on_device(): spatial.astype(jnp.float32) * scale  1.56 us

profile of v2, /device:TPU:1, one launch (start us, length us, event | category | flops | bytes accessed | tf_op | source)
XLA Modules:
  0.0 60.2 jit_solution(3536363639494270869)
XLA Ops:
  0.6 0.0 copy-start
  0.6 1.3 %copy-done = bf16[3,3,256,256]{3,2,1,0:T(8,128)(2,1)S(1)} copy-done((bf16[3,3,256,256]{3,2,1,0:T(8,128)(2,1)S(1)}, bf16[3,3,256,256]{3,2,1,0:T(8,128)(2,1)}, u32[]{:S(2)}) %copy-start) | copy-done | bytes 1179672
  1.9 0.0 copy-start.1
  1.9 0.9 %copy-done.1 = bf16[1,16,4,8,256]{4,3,2,1,0:T(8,128)(2,1)S(1)} copy-done((bf16[1,16,4,8,256]{4,3,2,1,0:T(8,128)(2,1)S(1)}, bf16[1,16,4,8,256]{4,3,2,1,0:T(8,128)(2,1)}, u32[]{:S(2)}) %copy-start.1) | copy-done | bytes 262168
  2.9 0.0 copy-start.2
  2.9 1.0 %copy-done.2 = bf16[3,256,256]{2,1,0:T(8,128)(2,1)S(1)} copy-done((bf16[3,256,256]{2,1,0:T(8,128)(2,1)S(1)}, bf16[3,256,256]{2,1,0:T(8,128)(2,1)}, u32[]{:S(2)}) %copy-start.2) | copy-done | bytes 393240
  3.9 0.0 copy-start.3
  3.9 0.9 %copy-done.3 = bf16[1,2,32,8,256]{4,3,2,1,0:T(8,128)(2,1)S(1)} copy-done((bf16[1,2,32,8,256]{4,3,2,1,0:T(8,128)(2,1)S(1)}, bf16[1,2,32,8,256]{4,3,2,1,0:T(8,128)(2,1)}, u32[]{:S(2)}) %copy-start.3) | copy-done | bytes 262168
  4.8 0.0 copy-start.4
  4.8 0.7 %copy-done.4 = f32[256]{0:T(256)S(1)} copy-done((f32[256]{0:T(256)S(1)}, f32[256]{0:T(256)}, u32[]{:S(2)}) %copy-start.4) | copy-done | bytes 1048
  5.5 0.0 copy-start.5
  5.5 0.7 %copy-done.5 = f32[256]{0:T(256)S(1)} copy-done((f32[256]{0:T(256)S(1)}, f32[256]{0:T(256)}, u32[]{:S(2)}) %copy-start.5) | copy-done | bytes 1048
  6.2 0.0 copy-start.6
  6.2 0.7 %copy-done.6 = s32[1,6]{1,0:T(1,128)S(1)} copy-done((s32[1,6]{1,0:T(1,128)S(1)}, s32[1,6]{1,0:T(1,128)}, u32[]{:S(2)}) %copy-start.6) | copy-done | bytes 48
  6.8 50.0 %shard_map.94 = (bf16[2,256,256]{2,1,0:T(8,128)(2,1)S(1)}, bf16[6,32,16,256]{3,2,1,0:T(8,128)(2,1)S(1)}) custom-call(s32[1,6]{1,0:T(1,128)S(1)} %copy-done.6, bf16[16,32,256]{2,1,0:T(8,128)(2,1)S(1)} %bitcast.14, bf16[16,4,8,256]{3,2,1,0:T(8,128)(2,1)S(1)} %bitcast.15, bf16[2,256,256]{2,1,0:T(8,128)(2,1)S(1)} %bitcast.17, f32[1,256]{1,0:T(1,128)S(1)} %bitcast.19, ...), custom_call_target="tpu_custom_call" | custom-call | tf_op jit(solution)/shard_map/pallas_call | solution.py:379
  56.8 0.1 slice.8
  57.0 1.6 %convert_multiply_fusion = f32[2304,256]{1,0:T(8,128)} fusion(bf16[2304,256]{1,0:T(8,128)(2,1)S(1)} %slice.8), kind=kLoop, calls=%fused_computation | loop fusion | flops 1179648 | bytes 3538944 | tf_op jit(solution)/shard_map/mul | solution.py:430
  58.5 0.9 %convert_multiply_fusion.1 = f32[768,256]{1,0:T(8,128)} fusion(bf16[768,256]{1,0:T(8,128)(2,1)S(1)} %slice.9), kind=kLoop, calls=%fused_computation.1 | loop fusion | flops 393216 | bytes 1179648 | tf_op jit(solution)/shard_map/mul | solution.py:431
  59.5 0.7 %copy.11 = bf16[1,2,32,8,256]{4,3,2,1,0:T(8,128)(2,1)} copy(bf16[1,2,32,8,256]{4,3,2,1,0:T(8,128)(2,1)S(1)} %bitcast.18) | data formatting | bytes 524288
  (1 shorter events, 0.0 us)
Async XLA Ops:
  0.6 1.3 %copy-start = (bf16[3,3,256,256]{3,2,1,0:T(8,128)(2,1)S(1)}, bf16[3,3,256,256]{3,2,1,0:T(8,128)(2,1)}, u32[]{:S(2)}) copy-start(bf16[3,3,256,256]{3,2,1,0:T(8,128)(2,1)} %param.11) | copy-start | bytes 3538948
  1.9 0.9 %copy-start.1 = (bf16[1,16,4,8,256]{4,3,2,1,0:T(8,128)(2,1)S(1)}, bf16[1,16,4,8,256]{4,3,2,1,0:T(8,128)(2,1)}, u32[]{:S(2)}) copy-start(bf16[1,16,4,8,256]{4,3,2,1,0:T(8,128)(2,1)} %param.7) | copy-start | bytes 786436
  2.9 1.0 %copy-start.2 = (bf16[3,256,256]{2,1,0:T(8,128)(2,1)S(1)}, bf16[3,256,256]{2,1,0:T(8,128)(2,1)}, u32[]{:S(2)}) copy-start(bf16[3,256,256]{2,1,0:T(8,128)(2,1)} %param.12) | copy-start | bytes 1179652
  3.9 0.9 %copy-start.3 = (bf16[1,2,32,8,256]{4,3,2,1,0:T(8,128)(2,1)S(1)}, bf16[1,2,32,8,256]{4,3,2,1,0:T(8,128)(2,1)}, u32[]{:S(2)}) copy-start(bf16[1,2,32,8,256]{4,3,2,1,0:T(8,128)(2,1)} %param.13) | copy-start | bytes 786436
  4.8 0.7 %copy-start.4 = (f32[256]{0:T(256)S(1)}, f32[256]{0:T(256)}, u32[]{:S(2)}) copy-start(f32[256]{0:T(256)} %param.9) | copy-start | bytes 3076
  5.5 0.7 %copy-start.5 = (f32[256]{0:T(256)S(1)}, f32[256]{0:T(256)}, u32[]{:S(2)}) copy-start(f32[256]{0:T(256)} %param.10) | copy-start | bytes 3076
  6.2 0.7 %copy-start.6 = (s32[1,6]{1,0:T(1,128)S(1)}, s32[1,6]{1,0:T(1,128)}, u32[]{:S(2)}) copy-start(s32[1,6]{1,0:T(1,128)} %lengths_ref.1) | copy-start | bytes 76

commit v3 on v2

--- a/solution.py
+++ b/solution.py
@@ -67,13 +67,13 @@
     tiles,
     width,
     lengths_ref,
-    video_ref,
+    video_hbm,
     strips_ref,
     cot_ref,
-    gain_ref,
-    bias_ref,
-    sw_ref,
-    tw_ref,
+    gain_hbm,
+    bias_hbm,
+    sw_hbm,
+    tw_hbm,
     out_ref,
     sum_ref,
     *scratch,
@@ -82,7 +82,8 @@
     mine, theirs, above, below, cot_rows, cols, early, late = scratch[:8]
     stat_send, stat_recv, halo_send, halo_recv, cot_send, cot_recv = scratch[8:14]
     enc_send, enc_recv, sends, recvs = scratch[14:18]
-    bufs = scratch[18:]
+    video_ref, gain_ref, bias_ref, sw_ref, tw_ref, load_sem = scratch[18:24]
+    bufs = scratch[24:]
     dp, me = lax.axis_index("dp"), lax.axis_index("tile")
     frames, cells, channels = video_ref.shape
     strip = cells // width
@@ -101,6 +102,25 @@
     for peer in greet:
         pl.semaphore_signal(barrier, inc=1, device_id=peer, device_id_type=MESH)
 
+    loads = [
+        pltpu.make_async_copy(src, dst, load_sem.at[k])
+        for k, (src, dst) in enumerate(
+            (
+                (video_hbm, video_ref),
+                (gain_hbm, gain_ref),
+                (bias_hbm, bias_ref),
+                (sw_hbm, sw_ref),
+                (tw_hbm, tw_ref),
+                (
+                    cot_ref.at[:, pl.ds(me * cells, cells)],
+                    cot_rows.at[pl.ds(me * frame_dev, frame_dev)],
+                ),
+            )
+        )
+    ]
+    for copy in loads:
+        copy.start()
+    loads[0].wait()
     values = video_ref[...].astype(f32)
     sums = jnp.concatenate(
         [jnp.sum(values, axis=1), jnp.sum(values * values, axis=1)], axis=0
@@ -141,7 +161,6 @@
         )
         copy.start()
         moves.append(copy)
-    cot_rows[pl.ds(me * frame_dev, frame_dev)] = cot_ref[:, pl.ds(me * cells, cells)]
 
     clip_a = pick_rows(lengths_ref, lax.broadcasted_iota(jnp.int32, (frames, frames), 0))
     clip_b = pick_rows(lengths_ref, lax.broadcasted_iota(jnp.int32, (frames, frames), 1))
@@ -164,6 +183,8 @@
         total = total + theirs[k]
     mean = dot32(same, total[:frames]) / count
     var = jnp.maximum(dot32(same, total[frames:]) / count - mean * mean, 0.0)
+    loads[1].wait()
+    loads[2].wait()
     mean = dot32(mean, widen)
     slope = dot32(lax.rsqrt(var + norm_eps), widen) * gain_ref[...]
     bias = bias_ref[...]
@@ -198,6 +219,7 @@
                 cols[f * cells : (f + 1) * cells, tap : tap + channels] = shifted[j][
                     i * width : i * width + cells
                 ].astype(bf16)
+    loads[3].wait()
     conv = jnp.dot(cols[...], sw_ref[...], preferred_element_type=f32)
     block = video_ref[...].astype(f32).reshape(rows, channels) + conv
     block = block.astype(bf16)
@@ -208,6 +230,7 @@
         span = slice(k * channels, (k + 1) * channels)
         early[:lag, span] = jnp.zeros((lag, channels), bf16)
         early[lag:, span] = (block[: rows - lag] * keeps[k][lag:]).astype(bf16)
+    loads[4].wait()
     lifted = jnp.dot(early[...], tw_ref[...], preferred_element_type=f32)
     enc = bufs[0]
     enc[...] = (block + lifted).astype(bf16).reshape(frames, cells, channels)
@@ -223,6 +246,7 @@
         moves.append(copy)
     out_ref[:, pl.ds(me * cells, cells)] = enc[pl.ds(me * frame_dev, frame_dev)]
 
+    loads[5].wait()
     for copy in moves[: tiles - 1]:
         copy.wait_recv()
     cot = cot_rows[...].reshape(rows, channels)
@@ -375,6 +399,12 @@
         dma((tiles - 1,)),
         dma((copies,)),
         dma((copies,)),
+        pltpu.VMEM(video.shape, bf16),
+        pltpu.VMEM(gain.shape, f32),
+        pltpu.VMEM(bias.shape, f32),
+        pltpu.VMEM(sw.shape, bf16),
+        pltpu.VMEM(tw.shape, bf16),
+        dma((6,)),
     ]
     return pl.pallas_call(
         functools.partial(block_kernel, dps, tiles, width),
@@ -382,20 +412,12 @@
             jax.ShapeDtypeStruct((frames // tiles, cells * tiles, channels), bf16),
             jax.ShapeDtypeStruct((chunks, pieces, depth, channels), bf16),
         ],
-        in_specs=[
-            pl.BlockSpec(memory_space=pltpu.SMEM),
-            vmem,
-            pl.BlockSpec(memory_space=pl.ANY),
-            vmem,
-            vmem,
-            vmem,
-            vmem,
-            vmem,
-        ],
+        in_specs=[pl.BlockSpec(memory_space=pltpu.SMEM)]
+        + [pl.BlockSpec(memory_space=pl.ANY)] * 7,
         out_specs=[vmem] * 2,
         scratch_shapes=scratch + bufs,
         compiler_params=pltpu.CompilerParams(
-            collective_id=0, has_side_effects=True, vmem_limit_bytes=48 << 20
+            collective_id=0, has_side_effects=True, vmem_limit_bytes=56 << 20
         ),
     )(lengths, video, strips, cot, gain, bias, sw, tw)
 

time: 60.5 us -> 56.3 us (0.931)
  local copies, waits for them, and re-layouts: 6.98 us -> 3.08 us
    unnamed x15 -> x3, local copies, waits for them, and re-layouts: 6.87 us -> 0.71 us
    slice x1, local copies, waits for them, and re-layouts: 0.08 us -> 1.35 us  [on_device(): total[:9 * channels]]
    slice x1, local copies, waits for them, and re-layouts: 0.03 us -> 1.02 us  [on_device(): total[9 * channels:]]
where the time goes in v3:
time: 56.3 us; the launch traced here: 56.1 us
  Pallas kernels  49.9 us (89%)
  local copies, waits for them, and re-layouts  3.08 us (5%)
  other arithmetic  2.49 us (4%)
  between operations  0.66 us (1%)
    pallas_call x1, Pallas kernels, residual_block(): pl.pallas_call(functools.partial(block_kernel, dps, tiles, width), out_sh...  49.9 us
    mul x1, other arithmetic, on_device(): spatial.astype(jnp.float32) * scale  1.56 us
    slice x1, local copies, waits for them, and re-layouts, on_device(): total[:9 * channels]  1.35 us

profile of v3, /device:TPU:1, one launch (start us, length us, event | category | flops | bytes accessed | tf_op | source)
XLA Modules:
  0.0 56.1 jit_solution(7215895177596251757)
XLA Ops:
  0.6 49.9 %shard_map.94 = (bf16[2,256,256]{2,1,0:T(8,128)(2,1)}, bf16[6,32,16,256]{3,2,1,0:T(8,128)(2,1)}) custom-call(s32[1,6]{1,0:T(1,128)} %lengths_ref.1, bf16[16,32,256]{2,1,0:T(8,128)(2,1)} %bitcast.15, bf16[16,4,8,256]{3,2,1,0:T(8,128)(2,1)} %bitcast.16, bf16[2,256,256]{2,1,0:T(8,128)(2,1)} %bitcast.19, f32[1,256]{1,0:T(1,128)} %bitcast.21, f32[1,256]{1,0:T(1,128)} %bitcast.22, ...), custom_call_target="tpu_custom_call" | custom-call | tf_op jit(solution)/shard_map/pallas_call | solution.py:409
  50.5 1.3 %slice.8 = bf16[2304,256]{1,0:T(8,128)(2,1)S(1)} slice(bf16[3072,256]{1,0:T(8,128)(2,1)} %bitcast.12), slice={[0:2304], [0:256]} | slice | bytes 2359296 | tf_op jit(solution)/shard_map/slice | solution.py:448
  51.8 1.0 %slice.9 = bf16[768,256]{1,0:T(8,128)(2,1)S(1)} slice(bf16[3072,256]{1,0:T(8,128)(2,1)} %bitcast.13), slice={[2304:3072], [0:256]} | slice | bytes 786432 | tf_op jit(solution)/shard_map/slice | solution.py:448
  52.9 0.0 copy-start
  52.9 1.6 %convert_multiply_fusion = f32[2304,256]{1,0:T(8,128)} fusion(bf16[2304,256]{1,0:T(8,128)(2,1)S(1)} %slice.8), kind=kLoop, calls=%fused_computation | loop fusion | flops 1179648 | bytes 3538944 | tf_op jit(solution)/shard_map/mul | solution.py:452
  54.4 0.9 %convert_multiply_fusion.1 = f32[768,256]{1,0:T(8,128)} fusion(bf16[768,256]{1,0:T(8,128)(2,1)S(1)} %slice.9), kind=kLoop, calls=%fused_computation.1 | loop fusion | flops 393216 | bytes 1179648 | tf_op jit(solution)/shard_map/mul | solution.py:453
  55.4 0.0 copy-done
  55.4 0.7 %copy.11 = bf16[1,2,32,8,256]{4,3,2,1,0:T(8,128)(2,1)} copy(bf16[1,2,32,8,256]{4,3,2,1,0:T(8,128)(2,1)S(1)} %bitcast.20) | data formatting | bytes 524288
Async XLA Ops:
  52.9 2.5 %copy-start = (bf16[2,256,256]{2,1,0:T(8,128)(2,1)S(1)}, bf16[2,256,256]{2,1,0:T(8,128)(2,1)}, u32[]{:S(2)}) copy-start(bf16[2,256,256]{2,1,0:T(8,128)(2,1)} %get-tuple-element.7) | copy-start | bytes 786436

commit v4 on v3

--- a/solution.py
+++ b/solution.py
@@ -417,7 +417,7 @@
         out_specs=[vmem] * 2,
         scratch_shapes=scratch + bufs,
         compiler_params=pltpu.CompilerParams(
-            collective_id=0, has_side_effects=True, vmem_limit_bytes=56 << 20
+            collective_id=0, has_side_effects=True, vmem_limit_bytes=48 << 20
         ),
     )(lengths, video, strips, cot, gain, bias, sw, tw)
 

time: 56.3 us -> 60.1 us (1.067)
  local copies, waits for them, and re-layouts: 3.08 us -> 6.98 us
    unnamed x3 -> x15, local copies, waits for them, and re-layouts: 0.71 us -> 6.87 us
    slice x1, local copies, waits for them, and re-layouts: 1.35 us -> 0.08 us  [on_device(): total[:9 * channels]]
    slice x1, local copies, waits for them, and re-layouts: 1.02 us -> 0.03 us  [on_device(): total[9 * channels:]]
where the time goes in v4:
time: 60.1 us; the launch traced here: 59.8 us
  Pallas kernels  49.6 us (83%)
  local copies, waits for them, and re-layouts  6.98 us (12%)
  other arithmetic  2.49 us (4%)
  between operations  0.67 us (1%)
    pallas_call x1, Pallas kernels, residual_block(): pl.pallas_call(functools.partial(block_kernel, dps, tiles, width), out_sh...  49.6 us
    unnamed x15, local copies, waits for them, and re-layouts  6.87 us
    mul x1, other arithmetic, on_device(): spatial.astype(jnp.float32) * scale  1.56 us

profile of v4, /device:TPU:1, one launch (start us, length us, event | category | flops | bytes accessed | tf_op | source)
XLA Modules:
  0.0 59.8 jit_solution(18217063985566452)
XLA Ops:
  0.6 0.0 copy-start
  0.6 1.3 %copy-done = bf16[3,3,256,256]{3,2,1,0:T(8,128)(2,1)S(1)} copy-done((bf16[3,3,256,256]{3,2,1,0:T(8,128)(2,1)S(1)}, bf16[3,3,256,256]{3,2,1,0:T(8,128)(2,1)}, u32[]{:S(2)}) %copy-start) | copy-done | bytes 1179672
  1.9 0.0 copy-start.1
  1.9 0.9 %copy-done.1 = bf16[1,16,4,8,256]{4,3,2,1,0:T(8,128)(2,1)S(1)} copy-done((bf16[1,16,4,8,256]{4,3,2,1,0:T(8,128)(2,1)S(1)}, bf16[1,16,4,8,256]{4,3,2,1,0:T(8,128)(2,1)}, u32[]{:S(2)}) %copy-start.1) | copy-done | bytes 262168
  2.9 0.0 copy-start.2
  2.9 1.0 %copy-done.2 = bf16[3,256,256]{2,1,0:T(8,128)(2,1)S(1)} copy-done((bf16[3,256,256]{2,1,0:T(8,128)(2,1)S(1)}, bf16[3,256,256]{2,1,0:T(8,128)(2,1)}, u32[]{:S(2)}) %copy-start.2) | copy-done | bytes 393240
  3.9 0.0 copy-start.3
  3.9 0.9 %copy-done.3 = bf16[1,2,32,8,256]{4,3,2,1,0:T(8,128)(2,1)S(1)} copy-done((bf16[1,2,32,8,256]{4,3,2,1,0:T(8,128)(2,1)S(1)}, bf16[1,2,32,8,256]{4,3,2,1,0:T(8,128)(2,1)}, u32[]{:S(2)}) %copy-start.3) | copy-done | bytes 262168
  4.8 0.0 copy-start.4
  4.8 0.7 %copy-done.4 = f32[256]{0:T(256)S(1)} copy-done((f32[256]{0:T(256)S(1)}, f32[256]{0:T(256)}, u32[]{:S(2)}) %copy-start.4) | copy-done | bytes 1048
  5.5 0.0 copy-start.5
  5.5 0.7 %copy-done.5 = f32[256]{0:T(256)S(1)} copy-done((f32[256]{0:T(256)S(1)}, f32[256]{0:T(256)}, u32[]{:S(2)}) %copy-start.5) | copy-done | bytes 1048
  6.2 0.0 copy-start.6
  6.2 0.7 %copy-done.6 = s32[1,6]{1,0:T(1,128)S(1)} copy-done((s32[1,6]{1,0:T(1,128)S(1)}, s32[1,6]{1,0:T(1,128)}, u32[]{:S(2)}) %copy-start.6) | copy-done | bytes 48
  6.8 49.6 %shard_map.94 = (bf16[2,256,256]{2,1,0:T(8,128)(2,1)S(1)}, bf16[6,32,16,256]{3,2,1,0:T(8,128)(2,1)S(1)}) custom-call(s32[1,6]{1,0:T(1,128)S(1)} %copy-done.6, bf16[16,32,256]{2,1,0:T(8,128)(2,1)S(1)} %bitcast.14, bf16[16,4,8,256]{3,2,1,0:T(8,128)(2,1)S(1)} %bitcast.15, bf16[2,256,256]{2,1,0:T(8,128)(2,1)S(1)} %bitcast.17, f32[1,256]{1,0:T(1,128)S(1)} %bitcast.19, ...), custom_call_target="tpu_custom_call" | custom-call | tf_op jit(solution)/shard_map/pallas_call | solution.py:409
  56.5 0.1 slice.8
  56.6 1.6 %convert_multiply_fusion = f32[2304,256]{1,0:T(8,128)} fusion(bf16[2304,256]{1,0:T(8,128)(2,1)S(1)} %slice.8), kind=kLoop, calls=%fused_computation | loop fusion | flops 1179648 | bytes 3538944 | tf_op jit(solution)/shard_map/mul | solution.py:452
  58.2 0.9 %convert_multiply_fusion.1 = f32[768,256]{1,0:T(8,128)} fusion(bf16[768,256]{1,0:T(8,128)(2,1)S(1)} %slice.9), kind=kLoop, calls=%fused_computation.1 | loop fusion | flops 393216 | bytes 1179648 | tf_op jit(solution)/shard_map/mul | solution.py:453
  59.1 0.7 %copy.11 = bf16[1,2,32,8,256]{4,3,2,1,0:T(8,128)(2,1)} copy(bf16[1,2,32,8,256]{4,3,2,1,0:T(8,128)(2,1)S(1)} %bitcast.18) | data formatting | bytes 524288
  (1 shorter events, 0.0 us)
Async XLA Ops:
  0.6 1.3 %copy-start = (bf16[3,3,256,256]{3,2,1,0:T(8,128)(2,1)S(1)}, bf16[3,3,256,256]{3,2,1,0:T(8,128)(2,1)}, u32[]{:S(2)}) copy-start(bf16[3,3,256,256]{3,2,1,0:T(8,128)(2,1)} %param.11) | copy-start | bytes 3538948
  1.9 0.9 %copy-start.1 = (bf16[1,16,4,8,256]{4,3,2,1,0:T(8,128)(2,1)S(1)}, bf16[1,16,4,8,256]{4,3,2,1,0:T(8,128)(2,1)}, u32[]{:S(2)}) copy-start(bf16[1,16,4,8,256]{4,3,2,1,0:T(8,128)(2,1)} %param.7) | copy-start | bytes 786436
  2.9 1.0 %copy-start.2 = (bf16[3,256,256]{2,1,0:T(8,128)(2,1)S(1)}, bf16[3,256,256]{2,1,0:T(8,128)(2,1)}, u32[]{:S(2)}) copy-start(bf16[3,256,256]{2,1,0:T(8,128)(2,1)} %param.12) | copy-start | bytes 1179652
  3.9 0.9 %copy-start.3 = (bf16[1,2,32,8,256]{4,3,2,1,0:T(8,128)(2,1)S(1)}, bf16[1,2,32,8,256]{4,3,2,1,0:T(8,128)(2,1)}, u32[]{:S(2)}) copy-start(bf16[1,2,32,8,256]{4,3,2,1,0:T(8,128)(2,1)} %param.13) | copy-start | bytes 786436
  4.8 0.7 %copy-start.4 = (f32[256]{0:T(256)S(1)}, f32[256]{0:T(256)}, u32[]{:S(2)}) copy-start(f32[256]{0:T(256)} %param.9) | copy-start | bytes 3076
  5.5 0.7 %copy-start.5 = (f32[256]{0:T(256)S(1)}, f32[256]{0:T(256)}, u32[]{:S(2)}) copy-start(f32[256]{0:T(256)} %param.10) | copy-start | bytes 3076
  6.2 0.7 %copy-start.6 = (s32[1,6]{1,0:T(1,128)S(1)}, s32[1,6]{1,0:T(1,128)}, u32[]{:S(2)}) copy-start(s32[1,6]{1,0:T(1,128)} %lengths_ref.1) | copy-start | bytes 76
